TPU v7x, 512 devices: a whole 4x4x16 slice. The times are simulated.
512 devices in a mesh: row: 32 (over x, y, core), col: 16 (over z).
Axes of the slice: x: 4, y: 4, z: 16, core: 2. Of those that a mesh axis runs over, the one named last changes fastest.
Arguments:
- diag_factor: float32 [1024, 1024], P('row', 'col'), may hold values from -1 to 2.5, as said below
- panel_factor: float32 [16384, 1024], P('row', 'col'), may hold values from -0.046875 to 0.046875
- left_factor: float32 [16384, 8192], P('row', 'col'), may hold values from -0.046875 to 0.046875
- pivot_factor: float32 [1024, 8192], P('row', 'col'), may hold values from -0.1875 to 0.1875
- panel_adjoint: float32 [16384, 1024], P('row', 'col'), may hold values from -6 to 6
- left_adjoint: float32 [16384, 8192], P('row', 'col'), may hold values from -6 to 6
- pivot_adjoint: float32 [1024, 8192], P('row', 'col'), may hold values from -6 to 6
- diag_adjoint: float32 [1024, 1024], P('row', 'col'), may hold values from -6 to 6
Outputs:
- solved_panel: float32 [16384, 1024], P('row', 'col')
- left_out: float32 [16384, 8192], P('row', 'col')
- pivot_out: float32 [1024, 8192], P('row', 'col')
- diag_out: float32 [1024, 1024], P('row', 'col')
Inputs may be any that keep to these rules, and one draw needn't show every extreme that they name: diag_factor is lower triangular: zero above the diagonal, diagonal entries at least 1.
All inputs are finite; a program needn't handle non-finite values.
Results may differ from a plain program's by a relative error of at most 0.000073.
Values sent between devices are 32-bit elements; how exact they have to be, the bound alone decides.
A program may use at most 64 MiB of HBM per device.

v0:
```python
import jax
import jax.numpy as jnp
from jax import lax
from jax.sharding import PartitionSpec as P


def right_solve(tile, source):
    return jax.scipy.linalg.solve_triangular(tile, source.T, trans="T", lower=True).T


def local(
    diag_factor,
    panel_factor,
    left_factor,
    pivot_factor,
    panel_adjoint,
    left_adjoint,
    pivot_adjoint,
    diag_adjoint,
):
    highest = lax.Precision.HIGHEST
    block_width = panel_adjoint.shape[1]
    my_col = lax.axis_index("col")
    my_row = lax.axis_index("row")
    column_block = lax.all_gather(diag_factor, "row", axis=0, tiled=True)
    whole_diag = lax.all_gather(column_block, "col", axis=1, tiled=True)
    full_rows = lax.all_gather(panel_adjoint, "col", axis=1, tiled=True)
    solved = right_solve(whole_diag, full_rows)
    solved_panel = lax.dynamic_slice_in_dim(solved, my_col * block_width, block_width, 1)
    picked = solved
    left_out = left_adjoint - jnp.dot(
        picked,
        lax.all_gather(pivot_factor, "row", axis=0, tiled=True),
        precision=highest,
        preferred_element_type=jnp.float32,
    )
    own_rows = diag_adjoint.shape[0]
    picked = solved
    pivot_sum = lax.psum_scatter(
        jnp.einsum("rk,rc->kc", picked, left_factor, precision=highest),
        "row",
        scatter_dimension=0,
        tiled=True,
    )
    picked = solved
    square_sum = lax.psum_scatter(
        jnp.einsum("rk,rc->kc", picked, panel_factor, precision=highest),
        "row",
        scatter_dimension=0,
        tiled=True,
    )
    pivot_out = pivot_adjoint - pivot_sum
    global_row = my_row * own_rows + lax.broadcasted_iota(jnp.int32, (own_rows, block_width), 0)
    global_col = my_col * block_width + lax.broadcasted_iota(jnp.int32, (own_rows, block_width), 1)
    diag_out = diag_adjoint - jnp.where(global_col <= global_row, square_sum, 0.0)
    return (solved_panel, left_out, pivot_out, diag_out)


def solution(mesh):
    in_specs = (
        P("row", "col"),
        P("row", "col"),
        P("row", "col"),
        P("row", "col"),
        P("row", "col"),
        P("row", "col"),
        P("row", "col"),
        P("row", "col"),
    )
    out_specs = (P("row", "col"), P("row", "col"), P("row", "col"), P("row", "col"))
    return jax.shard_map(local, mesh=mesh, in_specs=in_specs, out_specs=out_specs, check_vma=False)
```

profile of v0, /device:TPU:2, one launch (start us, length us, event | category | flops | bytes accessed | tf_op | source)
XLA Modules:
  0.0 463.6 jit_solution(8965409141635587499)
XLA Ops:
  7.2 27.8 %all_gather.12 = f32[1024,64]{1,0:T(8,128)S(1)} all-gather(f32[32,64]{1,0:T(8,128)} %param.8), channel_id=1, replica_groups=mesh['row'=32,'col'=16] {'row'}, dimensions={0}, use_global_device_ids=true | all-gather | bytes 270336 | tf_op jit(solution)/shard_map/all_gather | solution.py:25
  37.5 77.2 %all-gather.4.cloned.1.call-done = f32[1024,1024]{0,1:T(8,128)} async-done(((f32[1024,64]{0,1:T(8,128)}), f32[1024,1024]{0,1:T(8,128)}) %all-gather.4.cloned.1.call-update) | async-done | bytes 4194320 | tf_op jit(solution)/shard_map/all_gather | solution.py:26
  114.7 4.8 %fusion = f32[1024,1024]{0,1:T(8,128)} fusion(f32[1024,1024]{0,1:T(8,128)} %all-gather.4.cloned.1.call-done), kind=kLoop, calls=%fused_computation.3 | loop fusion | flops 2097152 | bytes 8388608 | tf_op jit(solution)/shard_map/jit(_solve_triangular)/triangular_solve | solution.py:8
  119.5 24.1 %while.1 = (s32[]{:T(128)}, f32[1024,1024]{0,1:T(8,128)}, s32[8,2]{0,1:T(2,128)S(1)}, f32[8,128,128]{2,1,0:T(8,128)S(1)}, s32[]{:T(128)}) while((s32[]{:T(128)}, f32[1024,1024]{0,1:T(8,128)}, s32[8,2]{0,1:T(2,128)S(1)}, f32[8,128,128]{2,1,0:T(8,128)S(1)}, s32[]{:T(128)}) %tuple.28), condition=%wide.while_cond, body=%wide.while_body.sunk | while | flops 2 | bytes 393321 | solution.py:8
  120.1 2.3 dynamic-slice.12
  123.1 2.3 dynamic-slice.12
  126.1 2.3 dynamic-slice.12
  129.1 2.3 dynamic-slice.12
  132.2 2.3 dynamic-slice.12
  135.2 2.3 dynamic-slice.12
  138.2 2.3 dynamic-slice.12
  141.2 2.2 dynamic-slice.12
  143.6 78.6 %custom-call.4 = f32[8,128,128]{1,2,0:T(8,128)S(1)} custom-call(f32[8,128,128]{2,1,0:T(8,128)S(1)} %get-tuple-element.11), custom_call_target="InvertDiagBlocksLowerTriangular" | custom-call | tf_op jit(solution)/shard_map/jit(_solve_triangular)/triangular_solve | solution.py:8
  222.2 1.5 fusion.19
  227.3 1.6 convolution_subtract_fusion.6
  229.3 1.7 convolution_subtract_fusion.7
  231.4 1.9 convolution_subtract_fusion.2
  233.8 2.0 convolution_subtract_fusion.5
  236.4 2.2 convolution_subtract_fusion.1
  240.1 2.6 fusion.36
  243.0 4.8 %fusion.35 = f32[1024,512]{1,0:T(8,128)} fusion(f32[1024,512]{1,0:T(8,128)S(1)} %constant_dynamic-update-slice_fusion.18, f32[512,512]{1,0:T(8,128)S(1)} %copy-done), kind=kOutput, calls=%fused_computation.85 | convolution fusion | flops 3221225472 | bytes 5242880 | tf_op jit(solution)/shard_map/rk,rc->kc/dot_general | solution.py:40
  248.5 6.3 %convolution_subtract_fusion = f32[512,512]{1,0:T(8,128)} fusion(f32[512,512]{1,0:T(8,128)} %param.13, f32[1024,512]{1,0:T(8,128)S(1)} %constant_dynamic-update-slice_fusion.18, f32[1024,512]{1,0:T(8,128)} %all-gather.8.cloned.1.call-done), kind=kOutput, calls=%fused_computation.4 | convolution fusion | flops 3221487616 | bytes 6291456 | tf_op jit(solution)/shard_map/dot_general | solution.py:31
  254.9 95.1 %reduce-scatter.5.cloned.1.call-done = f32[32,64]{1,0:T(8,128)} async-done(((f32[1024,64]{1,0:T(8,128)}), f32[32,64]{1,0:T(8,128)}) %reduce-scatter.5.cloned.1.call-update) | async-done | bytes 8208 | tf_op jit(solution)/shard_map/reduce_scatter | solution.py:46
  351.3 104.3 %reduce-scatter.3.cloned.1.call-done = f32[32,512]{1,0:T(8,128)} async-done(((f32[1024,512]{1,0:T(8,128)}), f32[32,512]{1,0:T(8,128)}) %reduce-scatter.3.cloned.1.call-update) | async-done | bytes 65552 | tf_op jit(solution)/shard_map/reduce_scatter | solution.py:39
  (96 shorter events, 18.6 us)
Async XLA Ops:
  7.2 235.8 %copy-start = (f32[512,512]{1,0:T(8,128)S(1)}, f32[512,512]{1,0:T(8,128)}, u32[]{:S(2)}) copy-start(f32[512,512]{1,0:T(8,128)} %param.10) | copy-start | bytes 3145732
  7.2 107.5 %all-gather.4.cloned.1.call-start = ((), (), s32[]{:S(2)}) async-start(), calls=%async_computation.2 | async-start | bytes 4456448 | tf_op jit(solution)/shard_map/all_gather | solution.py:26
  35.9 186.3 %all-gather.6.cloned.1.call-start = ((), (), s32[]{:S(2)}) async-start(), calls=%async_computation.3 | async-start | bytes 2228224 | tf_op jit(solution)/shard_map/all_gather | solution.py:27
  36.7 211.8 %all-gather.8.cloned.1.call-start = ((), (), s32[]{:S(2)}) async-start(), calls=%async_computation.4 | async-start | bytes 2162688 | tf_op jit(solution)/shard_map/all_gather | solution.py:33
  37.4 312.5 %reduce-scatter.5.cloned.1.call-start = ((), (), s32[]{:S(2)}) async-start(), calls=%async_computation.6 | async-start | bytes 540672 | tf_op jit(solution)/shard_map/reduce_scatter | solution.py:46
  222.2 13.7 %copy-start.2 = (f32[8,128,128]{1,2,0:T(8,128)}, f32[8,128,128]{1,2,0:T(8,128)S(1)}, u32[]{:S(2)}) copy-start(f32[8,128,128]{1,2,0:T(8,128)S(1)} %custom-call.4) | copy-start | bytes 1572868
  222.2 5.1 %copy-start.1 = (f32[512,1024]{0,1:T(8,128)S(1)}, f32[512,1024]{0,1:T(8,128)}, u32[]{:S(2)}) copy-start(f32[512,1024]{0,1:T(8,128)} %all-gather.6.cloned.1.call-done) | copy-start | bytes 6291460
  238.6 1.5 copy-start.3
  242.7 212.9 %reduce-scatter.3.cloned.1.call-start = ((), (), s32[]{:S(2)}) async-start(), calls=%async_computation.5 | async-start | bytes 2162688 | tf_op jit(solution)/shard_map/reduce_scatter | solution.py:39
  248.5 101.4 %copy-start.5 = (f32[32,64]{1,0:T(8,128)S(1)}, f32[32,64]{1,0:T(8,128)}, u32[]{:S(2)}) copy-start(f32[32,64]{1,0:T(8,128)} %param.15) | copy-start | bytes 24580
  248.5 207.1 %copy-start.4 = (f32[32,512]{1,0:T(8,128)S(1)}, f32[32,512]{1,0:T(8,128)}, u32[]{:S(2)}) copy-start(f32[32,512]{1,0:T(8,128)} %param.14) | copy-start | bytes 196612
Sparse Core Ops, SparseCore 0:
  36.0 78.6 all-gather.3
  116.8 70.5 all-gather.5
  190.5 55.6 all-gather.7
  250.3 99.5 reduce-scatter.4
  354.2 101.3 reduce-scatter.2
where the time goes:
time: 465 us; the launch traced here: 464 us
  waiting for transfers between devices  278 us (60%)
  other arithmetic  86.2 us (19%)
  matrix products  30.8 us (7%)
  blocking collectives  27.8 us (6%)
  local copies, waits for them, and re-layouts  25.9 us (6%)
  between operations  14.2 us (3%)
    reduce_scatter x1, waiting for transfers between devices, local(): lax.psum_scatter(jnp.einsum('rk,rc->kc', picked, left_factor, precision=h...  104 us
    reduce_scatter x1, waiting for transfers between devices, local(): lax.psum_scatter(jnp.einsum('rk,rc->kc', picked, panel_factor, precision=...  95.1 us
    another operation x3, other arithmetic, right_solve(): jax.scipy.linalg.solve_triangular(tile, source.T, trans='T', lower=True)  83.4 us
    all_gather x1, waiting for transfers between devices, local(): whole_diag = lax.all_gather(column_block, 'col', axis=1, tiled=True)  77.2 us
    all_gather x1, blocking collectives, local(): column_block = lax.all_gather(diag_factor, 'row', axis=0, tiled=True)  27.8 us
    another operation x40, local copies, waits for them, and re-layouts  23.8 us
    another operation x15, matrix products, right_solve(): jax.scipy.linalg.solve_triangular(tile, source.T, trans='T', lower=True)  17.1 us
  transfers between devices with their start and end apart: 5, of which 3 were waited for; matrix products, arithmetic and copies ran while one was open for 30% of the time, Pallas kernels for 0%

commit v1 on v0

--- a/solution.py
+++ b/solution.py
@@ -2,6 +2,12 @@
 import jax.numpy as jnp
 from jax import lax
 from jax.sharding import PartitionSpec as P
+
+
+def joined_along(tiles, dim):
+    shape = list(tiles.shape[1:])
+    shape[dim] *= tiles.shape[0]
+    return jnp.moveaxis(tiles, 0, dim).reshape(shape)
 
 
 def right_solve(tile, source):
@@ -23,7 +29,19 @@
     my_col = lax.axis_index("col")
     my_row = lax.axis_index("row")
     column_block = lax.all_gather(diag_factor, "row", axis=0, tiled=True)
-    whole_diag = lax.all_gather(column_block, "col", axis=1, tiled=True)
+    count = lax.axis_size("col")
+    pairs = [(i, (i + 1) % count) for i in range(count)]
+    back = [(b, a) for a, b in pairs]
+    lower, upper = ([], [])
+    for step in range(count - 1):
+        if step % 2 == 0:
+            lower.append(lax.ppermute(lower[-1] if lower else column_block, "col", pairs))
+        else:
+            upper.append(lax.ppermute(upper[-1] if upper else column_block, "col", back))
+    blocks = jnp.stack([*lower[::-1], column_block, *upper])
+    shift = lax.axis_index("col") - len(lower)
+    blocks = blocks[(jnp.arange(count) - shift) % count]
+    whole_diag = joined_along(blocks, 1)
     full_rows = lax.all_gather(panel_adjoint, "col", axis=1, tiled=True)
     solved = right_solve(whole_diag, full_rows)
     solved_panel = lax.dynamic_slice_in_dim(solved, my_col * block_width, block_width, 1)

time: 465 us -> 502 us (1.080)
  starting transfers between devices: 0.42 us -> 51.6 us
  waiting for transfers between devices: 278 us -> 236 us
  local copies, waits for them, and re-layouts: 25.9 us -> 52.5 us
    all_gather x1 -> x0, waiting for transfers between devices: 77.2 us -> none  [local(): whole_diag = lax.all_gather(column_block, 'col', axis=1, tiled=True)]
    ppermute x0 -> x15, starting transfers between devices: none -> 51.2 us  [the longest x7 35.9 us: local(): lax.ppermute(upper[-1] if upper else column_block, 'col', back)]
    ppermute x0 -> x15, waiting for transfers between devices: none -> 44.5 us  [the longest x8 44.5 us: local(): lax.ppermute(lower[-1] if lower else column_block, 'col', pairs)]
    unnamed x30 -> x47, local copies, waits for them, and re-layouts: 0.39 us -> 17 us
    reduce_scatter x1, waiting for transfers between devices: 95.1 us -> 86.8 us  [local(): lax.psum_scatter(jnp.einsum('rk,rc->kc', picked, panel_factor, precision=...]
    another operation x40 -> x41, local copies, waits for them, and re-layouts: 23.8 us -> 29.6 us
    gather x0 -> x1, local copies, waits for them, and re-layouts: none -> 5.03 us  [local(): blocks = blocks[(jnp.arange(count) - shift) % count]]
  transfers between devices with their start and end apart: 5 -> 19, of which waited for: 3 -> 10; matrix products, arithmetic and copies ran while one was open for 30% -> 34% of each run, Pallas kernels for 0% -> 0%
where the time goes in v1:
time: 502 us; the launch traced here: 500 us
  waiting for transfers between devices  236 us (47%)
  other arithmetic  87 us (17%)
  local copies, waits for them, and re-layouts  52.5 us (10%)
  starting transfers between devices  51.6 us (10%)
  matrix products  30.8 us (6%)
  blocking collectives  27.6 us (5%)
  between operations  14.4 us (3%)
    reduce_scatter x1, waiting for transfers between devices, local(): lax.psum_scatter(jnp.einsum('rk,rc->kc', picked, left_factor, precision=h...  104 us
    reduce_scatter x1, waiting for transfers between devices, local(): lax.psum_scatter(jnp.einsum('rk,rc->kc', picked, panel_factor, precision=...  86.8 us
    another operation x3, other arithmetic, right_solve(): jax.scipy.linalg.solve_triangular(tile, source.T, trans='T', lower=True)  84.1 us
    ppermute x8, waiting for transfers between devices, local(): lax.ppermute(lower[-1] if lower else column_block, 'col', pairs)  44.5 us
    ppermute x7, starting transfers between devices, local(): lax.ppermute(upper[-1] if upper else column_block, 'col', back)  35.9 us
    another operation x40, local copies, waits for them, and re-layouts  28.9 us
    all_gather x1, blocking collectives, local(): column_block = lax.all_gather(diag_factor, 'row', axis=0, tiled=True)  27.6 us
    another operation x15, matrix products, right_solve(): jax.scipy.linalg.solve_triangular(tile, source.T, trans='T', lower=True)  17.1 us
  transfers between devices with their start and end apart: 19, of which 10 were waited for; matrix products, arithmetic and copies ran while one was open for 34% of the time, Pallas kernels for 0%

profile of v1, /device:TPU:2, one launch (start us, length us, event | category | flops | bytes accessed | tf_op | source)
XLA Modules:
  0.0 500.4 jit_solution(3875449213080011782)
XLA Ops:
  8.0 27.6 %all_gather.9 = f32[1024,64]{1,0:T(8,128)S(1)} all-gather(f32[32,64]{1,0:T(8,128)} %param.8), channel_id=1, replica_groups=mesh['row'=32,'col'=16] {'row'}, dimensions={0}, use_global_device_ids=true | all-gather | bytes 270336 | tf_op jit(solution)/shard_map/all_gather | solution.py:31
  37.7 16.2 %collective-permute-done = f32[1024,64]{0,1:T(8,128)S(1)} collective-permute-done((f32[1024,64]{0,1:T(8,128)S(1)}, f32[1024,64]{0,1:T(8,128)S(1)}, u32[]{:S(2)}, u32[]{:S(2)}) %collective-permute-start) | collective-permute-done | bytes 262176 | tf_op jit(solution)/shard_map/ppermute | solution.py:38
  55.9 5.1 %collective-permute-start.8 = (f32[1024,64]{0,1:T(8,128)S(1)}, f32[1024,64]{0,1:T(8,128)S(1)}, u32[]{:S(2)}, u32[]{:S(2)}) collective-permute-start(f32[1024,64]{0,1:T(8,128)S(1)} %copy.16), channel_id=1, source_target_pairs={{1,0},{2,1},{3,2},{4,3},{5,4},{6,5},{7,6},{8,7},{9,8},{10,9},{11,1... | collective-permute-start | bytes 786440 | tf_op jit(solution)/shard_map/ppermute | solution.py:40
  61.0 8.1 %collective-permute-done.1 = f32[1024,64]{0,1:T(8,128)S(1)} collective-permute-done((f32[1024,64]{0,1:T(8,128)S(1)}, f32[1024,64]{0,1:T(8,128)S(1)}, u32[]{:S(2)}, u32[]{:S(2)}) %collective-permute-start.1) | collective-permute-done | bytes 262176 | tf_op jit(solution)/shard_map/ppermute | solution.py:38
  71.1 5.1 %collective-permute-start.9 = (f32[1024,64]{0,1:T(8,128)S(1)}, f32[1024,64]{0,1:T(8,128)S(1)}, u32[]{:S(2)}, u32[]{:S(2)}) collective-permute-start(f32[1024,64]{0,1:T(8,128)S(1)} %collective-permute-done.8), channel_id=1, source_target_pairs={{1,0},{2,1},{3,2},{4,3},{5,4},{6,5},{7,6},{8,7},{9,8},{10,9},{11,1... | collective-permute-start | bytes 786440 | tf_op jit(solution)/shard_map/ppermute | solution.py:40
  76.2 6.5 %collective-permute-done.2 = f32[1024,64]{0,1:T(8,128)S(1)} collective-permute-done((f32[1024,64]{0,1:T(8,128)S(1)}, f32[1024,64]{0,1:T(8,128)S(1)}, u32[]{:S(2)}, u32[]{:S(2)}) %collective-permute-start.2) | collective-permute-done | bytes 262176 | tf_op jit(solution)/shard_map/ppermute | solution.py:38
  84.6 5.1 %collective-permute-start.10 = (f32[1024,64]{0,1:T(8,128)S(1)}, f32[1024,64]{0,1:T(8,128)S(1)}, u32[]{:S(2)}, u32[]{:S(2)}) collective-permute-start(f32[1024,64]{0,1:T(8,128)S(1)} %collective-permute-done.9), channel_id=1, source_target_pairs={{1,0},{2,1},{3,2},{4,3},{5,4},{6,5},{7,6},{8,7},{9,8},{10,9},{11,1... | collective-permute-start | bytes 786440 | tf_op jit(solution)/shard_map/ppermute | solution.py:40
  89.8 3.4 collective-permute-done.3
  95.1 5.1 %collective-permute-start.11 = (f32[1024,64]{0,1:T(8,128)S(1)}, f32[1024,64]{0,1:T(8,128)S(1)}, u32[]{:S(2)}, u32[]{:S(2)}) collective-permute-start(f32[1024,64]{0,1:T(8,128)S(1)} %collective-permute-done.10), channel_id=1, source_target_pairs={{1,0},{2,1},{3,2},{4,3},{5,4},{6,5},{7,6},{8,7},{9,8},{10,9},{11,1... | collective-permute-start | bytes 786440 | tf_op jit(solution)/shard_map/ppermute | solution.py:40
  104.6 5.1 %collective-permute-start.12 = (f32[1024,64]{0,1:T(8,128)S(1)}, f32[1024,64]{0,1:T(8,128)}, u32[]{:S(2)}, u32[]{:S(2)}) collective-permute-start(f32[1024,64]{0,1:T(8,128)S(1)} %collective-permute-done.11), channel_id=1, source_target_pairs={{1,0},{2,1},{3,2},{4,3},{5,4},{6,5},{7,6},{8,7},{9,8},{10,9},{11,1... | collective-permute-start | bytes 786440 | tf_op jit(solution)/shard_map/ppermute | solution.py:40
  109.8 2.5 collective-permute-done.5
  114.3 5.1 %collective-permute-start.13 = (f32[1024,64]{0,1:T(8,128)}, f32[1024,64]{0,1:T(8,128)}, u32[]{:S(2)}, u32[]{:S(2)}) collective-permute-start(f32[1024,64]{0,1:T(8,128)} %collective-permute-done.12), channel_id=1, source_target_pairs={{1,0},{2,1},{3,2},{4,3},{5,4},{6,5},{7,6},{8,7},{9,8},{10,9},{11,1... | collective-permute-start | bytes 786440 | tf_op jit(solution)/shard_map/ppermute | solution.py:40
  119.4 2.6 collective-permute-done.6
  124.0 5.1 %collective-permute-start.14 = (f32[1024,64]{0,1:T(8,128)}, f32[1024,64]{0,1:T(8,128)S(1)}, u32[]{:S(2)}, u32[]{:S(2)}) collective-permute-start(f32[1024,64]{0,1:T(8,128)} %collective-permute-done.13), channel_id=1, source_target_pairs={{1,0},{2,1},{3,2},{4,3},{5,4},{6,5},{7,6},{8,7},{9,8},{10,9},{11,1... | collective-permute-start | bytes 786440 | tf_op jit(solution)/shard_map/ppermute | solution.py:40
  129.2 2.6 collective-permute-done.7
  149.1 5.0 %gather_fusion = f32[16,1024,64]{1,2,0:T(8,128)} fusion(f32[16,1024,64]{1,2,0:T(8,128)} %bitcast_dynamic-update-slice_fusion.1, s32[1024]{0:T(1024)S(1)} %pad_clamp_fusion), kind=kCustom, calls=%fused_computation | custom fusion | bytes 8388672 | tf_op jit(solution)/shard_map/gather | solution.py:43
  154.1 4.7 bitcast_select_fusion
  158.9 29.0 %while.1 = (s32[]{:T(128)}, f32[1024,1024]{0,1:T(8,128)}, s32[8,2]{0,1:T(2,128)S(1)}, f32[8,128,128]{2,1,0:T(8,128)}, s32[]{:T(128)}) while((s32[]{:T(128)}, f32[1024,1024]{0,1:T(8,128)}, s32[8,2]{0,1:T(2,128)S(1)}, f32[8,128,128]{2,1,0:T(8,128)}, s32[]{:T(128)}) %tuple.29), condition=%wide.while_cond, body=%wide.while_body.sunk | while | flops 2 | bytes 393829 | solution.py:14
  187.8 79.4 %custom-call.4 = f32[8,128,128]{1,2,0:T(8,128)S(1)} custom-call(f32[8,128,128]{2,1,0:T(8,128)} %get-tuple-element.11), custom_call_target="InvertDiagBlocksLowerTriangular" | custom-call | tf_op jit(solution)/shard_map/jit(_solve_triangular)/triangular_solve | solution.py:14
  285.2 2.6 fusion.37
  288.0 4.8 fusion.36
  293.6 6.4 %convolution_subtract_fusion = f32[512,512]{1,0:T(8,128)} fusion(f32[512,512]{1,0:T(8,128)} %param.13, f32[1024,512]{1,0:T(8,128)S(1)} %constant_dynamic-update-slice_fusion.18, f32[1024,512]{1,0:T(8,128)} %all-gather.5.cloned.1.call-done), kind=kOutput, calls=%fused_computation.5 | convolution fusion | flops 3221487616 | bytes 6291456 | tf_op jit(solution)/shard_map/dot_general | solution.py:49
  299.9 86.8 %reduce-scatter.5.cloned.1.call-done = f32[32,64]{1,0:T(8,128)} async-done(((f32[1024,64]{1,0:T(8,128)}), f32[32,64]{1,0:T(8,128)}) %reduce-scatter.5.cloned.1.call-update) | async-done | bytes 8208 | tf_op jit(solution)/shard_map/reduce_scatter | solution.py:64
  388.1 104.3 %reduce-scatter.3.cloned.1.call-done = f32[32,512]{1,0:T(8,128)} async-done(((f32[1024,512]{1,0:T(8,128)}), f32[32,512]{1,0:T(8,128)}) %reduce-scatter.3.cloned.1.call-update) | async-done | bytes 65552 | tf_op jit(solution)/shard_map/reduce_scatter | solution.py:57
  (144 shorter events, 86.3 us)
Async XLA Ops:
  7.2 280.9 %copy-start = (f32[512,512]{1,0:T(8,128)S(1)}, f32[512,512]{1,0:T(8,128)}, u32[]{:S(2)}) copy-start(f32[512,512]{1,0:T(8,128)} %param.10) | copy-start | bytes 3145732
  7.2 260.1 %all-gather.3.cloned.1.call-start = ((), (), s32[]{:S(2)}) async-start(), calls=%async_computation.2 | async-start | bytes 2228224 | tf_op jit(solution)/shard_map/all_gather | solution.py:45
  7.9 285.7 %all-gather.5.cloned.1.call-start = ((), (), s32[]{:S(2)}) async-start(), calls=%async_computation.3 | async-start | bytes 2162688 | tf_op jit(solution)/shard_map/all_gather | solution.py:51
  35.8 18.2 %collective-permute-start = (f32[1024,64]{0,1:T(8,128)S(1)}, f32[1024,64]{0,1:T(8,128)S(1)}, u32[]{:S(2)}, u32[]{:S(2)}) collective-permute-start(f32[1024,64]{0,1:T(8,128)S(1)} %copy.16), channel_id=1, source_target_pairs={{0,1},{1,2},{2,3},{3,4},{4,5},{5,6},{6,7},{7,8},{8,9},{9,10},{10,1... | collective-permute-start | bytes 786440 | tf_op jit(solution)/shard_map/ppermute | solution.py:38
  54.0 15.2 %collective-permute-start.1 = (f32[1024,64]{0,1:T(8,128)S(1)}, f32[1024,64]{0,1:T(8,128)S(1)}, u32[]{:S(2)}, u32[]{:S(2)}) collective-permute-start(f32[1024,64]{0,1:T(8,128)S(1)} %collective-permute-done), channel_id=1, source_target_pairs={{0,1},{1,2},{2,3},{3,4},{4,5},{5,6},{6,7},{7,8},{8,9},{9,10},{10,1... | collective-permute-start | bytes 786440 | tf_op jit(solution)/shard_map/ppermute | solution.py:38
  55.9 15.2 %collective-permute-start.8 = (f32[1024,64]{0,1:T(8,128)S(1)}, f32[1024,64]{0,1:T(8,128)S(1)}, u32[]{:S(2)}, u32[]{:S(2)}) collective-permute-start(f32[1024,64]{0,1:T(8,128)S(1)} %copy.16), channel_id=1, source_target_pairs={{1,0},{2,1},{3,2},{4,3},{5,4},{6,5},{7,6},{8,7},{9,8},{10,9},{11,1... | collective-permute-start | bytes 786440 | tf_op jit(solution)/shard_map/ppermute | solution.py:40
  69.2 13.6 %collective-permute-start.2 = (f32[1024,64]{0,1:T(8,128)S(1)}, f32[1024,64]{0,1:T(8,128)S(1)}, u32[]{:S(2)}, u32[]{:S(2)}) collective-permute-start(f32[1024,64]{0,1:T(8,128)S(1)} %collective-permute-done.1), channel_id=1, source_target_pairs={{0,1},{1,2},{2,3},{3,4},{4,5},{5,6},{6,7},{7,8},{8,9},{9,10},{10,1... | collective-permute-start | bytes 786440 | tf_op jit(solution)/shard_map/ppermute | solution.py:38
  71.1 13.6 %collective-permute-start.9 = (f32[1024,64]{0,1:T(8,128)S(1)}, f32[1024,64]{0,1:T(8,128)S(1)}, u32[]{:S(2)}, u32[]{:S(2)}) collective-permute-start(f32[1024,64]{0,1:T(8,128)S(1)} %collective-permute-done.8), channel_id=1, source_target_pairs={{1,0},{2,1},{3,2},{4,3},{5,4},{6,5},{7,6},{8,7},{9,8},{10,9},{11,1... | collective-permute-start | bytes 786440 | tf_op jit(solution)/shard_map/ppermute | solution.py:40
  82.7 10.5 %collective-permute-start.3 = (f32[1024,64]{0,1:T(8,128)S(1)}, f32[1024,64]{0,1:T(8,128)S(1)}, u32[]{:S(2)}, u32[]{:S(2)}) collective-permute-start(f32[1024,64]{0,1:T(8,128)S(1)} %collective-permute-done.2), channel_id=1, source_target_pairs={{0,1},{1,2},{2,3},{3,4},{4,5},{5,6},{6,7},{7,8},{8,9},{9,10},{10,1... | collective-permute-start | bytes 786440 | tf_op jit(solution)/shard_map/ppermute | solution.py:38
  84.6 10.5 %collective-permute-start.10 = (f32[1024,64]{0,1:T(8,128)S(1)}, f32[1024,64]{0,1:T(8,128)S(1)}, u32[]{:S(2)}, u32[]{:S(2)}) collective-permute-start(f32[1024,64]{0,1:T(8,128)S(1)} %collective-permute-done.9), channel_id=1, source_target_pairs={{1,0},{2,1},{3,2},{4,3},{5,4},{6,5},{7,6},{8,7},{9,8},{10,9},{11,1... | collective-permute-start | bytes 786440 | tf_op jit(solution)/shard_map/ppermute | solution.py:40
  93.2 9.5 %collective-permute-start.4 = (f32[1024,64]{0,1:T(8,128)S(1)}, f32[1024,64]{0,1:T(8,128)S(1)}, u32[]{:S(2)}, u32[]{:S(2)}) collective-permute-start(f32[1024,64]{0,1:T(8,128)S(1)} %collective-permute-done.3), channel_id=1, source_target_pairs={{0,1},{1,2},{2,3},{3,4},{4,5},{5,6},{6,7},{7,8},{8,9},{9,10},{10,1... | collective-permute-start | bytes 786440 | tf_op jit(solution)/shard_map/ppermute | solution.py:38
  95.1 9.5 %collective-permute-start.11 = (f32[1024,64]{0,1:T(8,128)S(1)}, f32[1024,64]{0,1:T(8,128)S(1)}, u32[]{:S(2)}, u32[]{:S(2)}) collective-permute-start(f32[1024,64]{0,1:T(8,128)S(1)} %collective-permute-done.10), channel_id=1, source_target_pairs={{1,0},{2,1},{3,2},{4,3},{5,4},{6,5},{7,6},{8,7},{9,8},{10,9},{11,1... | collective-permute-start | bytes 786440 | tf_op jit(solution)/shard_map/ppermute | solution.py:40
  102.7 9.6 %collective-permute-start.5 = (f32[1024,64]{0,1:T(8,128)S(1)}, f32[1024,64]{0,1:T(8,128)}, u32[]{:S(2)}, u32[]{:S(2)}) collective-permute-start(f32[1024,64]{0,1:T(8,128)S(1)} %collective-permute-done.4), channel_id=1, source_target_pairs={{0,1},{1,2},{2,3},{3,4},{4,5},{5,6},{6,7},{7,8},{8,9},{9,10},{10,1... | collective-permute-start | bytes 786440 | tf_op jit(solution)/shard_map/ppermute | solution.py:38
  104.6 9.6 %collective-permute-start.12 = (f32[1024,64]{0,1:T(8,128)S(1)}, f32[1024,64]{0,1:T(8,128)}, u32[]{:S(2)}, u32[]{:S(2)}) collective-permute-start(f32[1024,64]{0,1:T(8,128)S(1)} %collective-permute-done.11), channel_id=1, source_target_pairs={{1,0},{2,1},{3,2},{4,3},{5,4},{6,5},{7,6},{8,7},{9,8},{10,9},{11,1... | collective-permute-start | bytes 786440 | tf_op jit(solution)/shard_map/ppermute | solution.py:40
  112.2 9.8 %collective-permute-start.6 = (f32[1024,64]{0,1:T(8,128)}, f32[1024,64]{0,1:T(8,128)}, u32[]{:S(2)}, u32[]{:S(2)}) collective-permute-start(f32[1024,64]{0,1:T(8,128)} %collective-permute-done.5), channel_id=1, source_target_pairs={{0,1},{1,2},{2,3},{3,4},{4,5},{5,6},{6,7},{7,8},{8,9},{9,10},{10,1... | collective-permute-start | bytes 786440 | tf_op jit(solution)/shard_map/ppermute | solution.py:38
  114.2 272.5 %reduce-scatter.5.cloned.1.call-start = ((), (), s32[]{:S(2)}) async-start(), calls=%async_computation.5 | async-start | bytes 540672 | tf_op jit(solution)/shard_map/reduce_scatter | solution.py:64
  114.3 9.8 %collective-permute-start.13 = (f32[1024,64]{0,1:T(8,128)}, f32[1024,64]{0,1:T(8,128)}, u32[]{:S(2)}, u32[]{:S(2)}) collective-permute-start(f32[1024,64]{0,1:T(8,128)} %collective-permute-done.12), channel_id=1, source_target_pairs={{1,0},{2,1},{3,2},{4,3},{5,4},{6,5},{7,6},{8,7},{9,8},{10,9},{11,1... | collective-permute-start | bytes 786440 | tf_op jit(solution)/shard_map/ppermute | solution.py:40
  122.0 9.8 %collective-permute-start.7 = (f32[1024,64]{0,1:T(8,128)}, f32[1024,64]{0,1:T(8,128)}, u32[]{:S(2)}, u32[]{:S(2)}) collective-permute-start(f32[1024,64]{0,1:T(8,128)} %collective-permute-done.6), channel_id=1, source_target_pairs={{0,1},{1,2},{2,3},{3,4},{4,5},{5,6},{6,7},{7,8},{8,9},{9,10},{10,1... | collective-permute-start | bytes 786440 | tf_op jit(solution)/shard_map/ppermute | solution.py:38
  124.0 24.4 %collective-permute-start.14 = (f32[1024,64]{0,1:T(8,128)}, f32[1024,64]{0,1:T(8,128)S(1)}, u32[]{:S(2)}, u32[]{:S(2)}) collective-permute-start(f32[1024,64]{0,1:T(8,128)} %collective-permute-done.13), channel_id=1, source_target_pairs={{1,0},{2,1},{3,2},{4,3},{5,4},{6,5},{7,6},{8,7},{9,8},{10,9},{11,1... | collective-permute-start | bytes 786440 | tf_op jit(solution)/shard_map/ppermute | solution.py:40
  267.2 13.7 %copy-start.2 = (f32[8,128,128]{1,2,0:T(8,128)}, f32[8,128,128]{1,2,0:T(8,128)S(1)}, u32[]{:S(2)}) copy-start(f32[8,128,128]{1,2,0:T(8,128)S(1)} %custom-call.4) | copy-start | bytes 1572868
  267.3 5.1 %copy-start.1 = (f32[512,1024]{0,1:T(8,128)S(1)}, f32[512,1024]{0,1:T(8,128)}, u32[]{:S(2)}) copy-start(f32[512,1024]{0,1:T(8,128)} %all-gather.3.cloned.1.call-done) | copy-start | bytes 6291460
  287.8 204.6 %reduce-scatter.3.cloned.1.call-start = ((), (), s32[]{:S(2)}) async-start(), calls=%async_computation.4 | async-start | bytes 2162688 | tf_op jit(solution)/shard_map/reduce_scatter | solution.py:57
  293.6 93.1 %copy-start.6 = (f32[32,64]{1,0:T(8,128)S(1)}, f32[32,64]{1,0:T(8,128)}, u32[]{:S(2)}) copy-start(f32[32,64]{1,0:T(8,128)} %param.15) | copy-start | bytes 24580
  293.6 198.8 %copy-start.5 = (f32[32,512]{1,0:T(8,128)S(1)}, f32[32,512]{1,0:T(8,128)}, u32[]{:S(2)}) copy-start(f32[32,512]{1,0:T(8,128)} %param.14) | copy-start | bytes 196612
  (2 other events, 3.4 us)
Sparse Core Ops, SparseCore 0:
  10.1 80.8 all-gather.2
  114.3 58.1 all-gather.4
  287.9 98.7 reduce-scatter.4
  391.0 101.3 reduce-scatter.2
